TPU v7x, 32 devices: a whole 2x2x4 slice. The times are simulated.
32 devices in a mesh: inline: 8 (over z, core), xline: 4 (over y, x).
Axes of the slice: x: 2, y: 2, z: 4, core: 2. Of those that a mesh axis runs over, the one named last changes fastest.
Arguments:
- probes: float32 [2, 128, 128, 128], P(None, 'inline', 'xline'), may hold values from -6 to 6
- diffusion: bfloat16 [3, 128, 128, 128], P(None, 'inline', 'xline'), may hold values from -1 to 1, as said below
- wavelet: float32 [41], replicated, may hold values from -1 to 1
Outputs:
- iterate: float32 [2, 128, 128, 128], P(None, 'inline', 'xline')
Inputs may be any that keep to these rules, and one draw needn't show every extreme that they name: `diffusion`: components 0 and 2 are positive; component 1 lies within nine tenths of the root of their product in magnitude.
All inputs are finite; a program needn't handle non-finite values.
Results may differ from a plain program's by a relative error of at most 0.0003.
Values may be sent and summed in bfloat16 or wider, within the bound.
A program may use at most 64 MiB of HBM per device.

v0:
```python
import jax
import jax.numpy as jnp
from jax import lax
from jax.sharding import PartitionSpec as P

HALF = 20
PAIRS = 3


def with_halo(block, sides, width):
    for axis, dim in sides:
        count = lax.axis_size(axis)
        forward = [(i, i + 1) for i in range(count - 1)]
        backward = [(target, source) for source, target in forward]
        low = lax.ppermute(
            lax.slice_in_dim(block, block.shape[dim] - width, None, axis=dim), axis, forward
        )
        high = lax.ppermute(lax.slice_in_dim(block, 0, width, axis=dim), axis, backward)
        block = jnp.concatenate([low, block, high], axis=dim)
    return block


def wavelet_matrix(wavelet, samples):
    offset = jnp.arange(samples)[None, :] - jnp.arange(samples)[:, None] + HALF
    onehot = (offset[:, :, None] == jnp.arange(2 * HALF + 1)[None, None, :]).astype(jnp.float32)
    return jnp.einsum("stk,k->st", onehot, wavelet, precision=lax.Precision.HIGHEST)


def apply_data(volume, matrices):
    shape = volume.shape
    trace_rows = volume.reshape(-1, shape[-1])
    for matrix in matrices:
        trace_rows = jnp.dot(trace_rows, matrix, precision=lax.Precision.HIGHEST)
    return trace_rows.reshape(shape)


def regularize(extended, tensor):
    middle = extended[:, :-1, :-1]
    step_in = extended[:, 1:, :-1] - middle
    step_x = extended[:, :-1, 1:] - middle
    flux_in = tensor[0] * step_in + tensor[1] * step_x
    flux_x = tensor[1] * step_in + tensor[2] * step_x
    return flux_in[:, :-1, 1:] - flux_in[:, 1:, 1:] + (flux_x[:, 1:, :-1] - flux_x[:, 1:, 1:])


def per_device(probes, diffusion, wavelet):
    samples = probes.shape[-1]
    wavelet_band = wavelet_matrix(wavelet, samples)
    matrices = (wavelet_band, wavelet_band.T)
    inline_cells = probes.shape[1]
    xline_cells = probes.shape[2]
    margin = with_halo(diffusion, (("inline", 1), ("xline", 2)), 2).astype(jnp.float32)
    place_in = lax.axis_index("inline") * inline_cells + jnp.arange(
        -1, inline_cells + 1, dtype=jnp.int32
    )
    place_x = lax.axis_index("xline") * xline_cells + jnp.arange(
        -1, xline_cells + 1, dtype=jnp.int32
    )
    inside_in = (place_in >= 0) & (place_in < inline_cells * lax.axis_size("inline"))
    inside_x = (place_x >= 0) & (place_x < xline_cells * lax.axis_size("xline"))
    inside = inside_in[None, :, None, None] & inside_x[None, None, :, None]
    outer_tensor = margin[:, :-1, :-1]
    inner_tensor = margin[:, 1:-2, 1:-2]
    result = probes
    for turn in range(PAIRS):
        extended = with_halo(result, (("inline", 1), ("xline", 2)), 2)
        centre = extended[:, 1:-1, 1:-1]
        first_pass = centre - 0.25 * (
            apply_data(centre, matrices) + regularize(extended, outer_tensor)
        )
        first_pass = jnp.where(inside, first_pass, jnp.float32(0.0))
        inner = first_pass[:, 1:-1, 1:-1]
        result = inner - 0.25 * (apply_data(inner, matrices) + regularize(first_pass, inner_tensor))
    return result


def solution(mesh):
    return jax.shard_map(
        per_device,
        mesh=mesh,
        in_specs=(P(None, "inline", "xline", None), P(None, "inline", "xline", None), P()),
        out_specs=P(None, "inline", "xline", None),
        check_vma=False,
    )
```

profile of v0, /device:TPU:1, one launch (start us, length us, event | category | flops | bytes accessed | tf_op | source)
XLA Modules:
  0.0 102.6 jit_solution(1601021043442517381)
XLA Ops:
  0.0 0.8 fusion.35
  0.8 2.0 %collective-permute-start.5 = (bf16[3,2,32,128]{3,2,1,0:T(8,128)(2,1)S(1)}, bf16[3,2,32,128]{3,2,1,0:T(8,128)(2,1)S(1)}, u32[]{:S(2)}, u32[]{:S(2)}) collective-permute-start(bf16[3,2,32,128]{3,2,1,0:T(8,128)(2,1)S(1)} %get-tuple-element.37), channel_id=1, source_target_pairs={{4,0},{8,4},{12,8},{16,12},{20,16},{24,20},{28,24},{5,1},{9,5},{13... | collective-permute-start | bytes 147464 | tf_op jit(solution)/shard_map/ppermute | solution.py:18
  2.8 4.5 %collective-permute-start.4 = (bf16[3,2,32,128]{3,2,1,0:T(8,128)(2,1)S(1)}, bf16[3,2,32,128]{3,2,1,0:T(8,128)(2,1)S(1)}, u32[]{:S(2)}, u32[]{:S(2)}) collective-permute-start(bf16[3,2,32,128]{3,2,1,0:T(8,128)(2,1)S(1)} %get-tuple-element.38), channel_id=1, source_target_pairs={{0,4},{4,8},{8,12},{12,16},{16,20},{20,24},{24,28},{1,5},{5,9},{9,... | collective-permute-start | bytes 147464 | tf_op jit(solution)/shard_map/ppermute | solution.py:15
  7.4 0.9 fusion.33
  8.3 1.9 %collective-permute-start.1 = (f32[2,2,32,128]{3,2,1,0:T(8,128)S(1)}, f32[2,2,32,128]{3,2,1,0:T(8,128)S(1)}, u32[]{:S(2)}, u32[]{:S(2)}) collective-permute-start(f32[2,2,32,128]{3,2,1,0:T(8,128)S(1)} %get-tuple-element.33), channel_id=1, source_target_pairs={{4,0},{8,4},{12,8},{16,12},{20,16},{24,20},{28,24},{5,1},{9,5},{13... | collective-permute-start | bytes 196616 | tf_op jit(solution)/shard_map/ppermute | solution.py:18
  10.2 3.6 %collective-permute-start = (f32[2,2,32,128]{3,2,1,0:T(8,128)S(1)}, f32[2,2,32,128]{3,2,1,0:T(8,128)S(1)}, u32[]{:S(2)}, u32[]{:S(2)}) collective-permute-start(f32[2,2,32,128]{3,2,1,0:T(8,128)S(1)} %get-tuple-element.34), channel_id=1, source_target_pairs={{0,4},{4,8},{8,12},{12,16},{16,20},{20,24},{24,28},{1,5},{5,9},{9,... | collective-permute-start | bytes 196616 | tf_op jit(solution)/shard_map/ppermute | solution.py:15
  14.3 1.6 %fusion = f32[1,128,128]{2,0,1:T(1,128)S(1)} fusion(pred[128,128,41]{1,0,2:T(32,128)(4,1)S(1)} %iota_compare_fusion, f32[41]{0:T(128)S(1)} %copy-done), kind=kOutput, calls=%fused_computation | convolution fusion | flops 8060928 | bytes 737444 | tf_op jit(solution)/shard_map/stk,k->st/dot_general | solution.py:26
  16.2 3.1 %collective-permute-start.6 = (bf16[3,20,2,128]{3,2,1,0:T(2,128)(2,1)S(1)}, bf16[3,20,2,128]{3,2,1,0:T(2,128)(2,1)S(1)}, u32[]{:S(2)}, u32[]{:S(2)}) collective-permute-start(bf16[3,20,2,128]{3,2,1,0:T(2,128)(2,1)S(1)} %get-tuple-element.35), channel_id=1, source_target_pairs={{0,1},{1,2},{2,3},{4,5},{5,6},{6,7},{8,9},{9,10},{10,11},{12,13},{... | collective-permute-start | bytes 92168 | tf_op jit(solution)/shard_map/ppermute | solution.py:15
  19.3 1.3 %collective-permute-start.7 = (bf16[3,20,2,128]{3,2,1,0:T(2,128)(2,1)S(1)}, bf16[3,20,2,128]{3,2,1,0:T(2,128)(2,1)S(1)}, u32[]{:S(2)}, u32[]{:S(2)}) collective-permute-start(bf16[3,20,2,128]{3,2,1,0:T(2,128)(2,1)S(1)} %get-tuple-element.36), channel_id=1, source_target_pairs={{1,0},{2,1},{3,2},{5,4},{6,5},{7,6},{9,8},{10,9},{11,10},{13,12},{... | collective-permute-start | bytes 92168 | tf_op jit(solution)/shard_map/ppermute | solution.py:18
  20.8 4.0 %collective-permute-start.2 = (f32[2,20,2,128]{3,2,1,0:T(2,128)S(1)}, f32[2,20,2,128]{3,2,1,0:T(2,128)S(1)}, u32[]{:S(2)}, u32[]{:S(2)}) collective-permute-start(f32[2,20,2,128]{3,2,1,0:T(2,128)S(1)} %get-tuple-element.27), channel_id=1, source_target_pairs={{0,1},{1,2},{2,3},{4,5},{5,6},{6,7},{8,9},{9,10},{10,11},{12,13},{... | collective-permute-start | bytes 122888 | tf_op jit(solution)/shard_map/ppermute | solution.py:15
  24.8 1.3 %collective-permute-start.3 = (f32[2,20,2,128]{3,2,1,0:T(2,128)S(1)}, f32[2,20,2,128]{3,2,1,0:T(2,128)S(1)}, u32[]{:S(2)}, u32[]{:S(2)}) collective-permute-start(f32[2,20,2,128]{3,2,1,0:T(2,128)S(1)} %get-tuple-element.28), channel_id=1, source_target_pairs={{1,0},{2,1},{3,2},{5,4},{6,5},{7,6},{9,8},{10,9},{11,10},{13,12},{... | collective-permute-start | bytes 122888 | tf_op jit(solution)/shard_map/ppermute | solution.py:18
  26.6 3.9 %collective-permute-done.3 = f32[2,20,2,128]{3,2,1,0:T(2,128)S(1)} collective-permute-done((f32[2,20,2,128]{3,2,1,0:T(2,128)S(1)}, f32[2,20,2,128]{3,2,1,0:T(2,128)S(1)}, u32[]{:S(2)}, u32[]{:S(2)}) %collective-permute-start.3) | collective-permute-done | bytes 40992 | tf_op jit(solution)/shard_map/ppermute | solution.py:18
  30.6 0.9 slice.308
  31.6 2.0 %reshape.101 = f32[1224,128]{1,0:T(8,128)} reshape(f32[2,18,34,128]{3,2,1,0:T(8,128)} %slice.308) | data formatting | bytes 1253376 | tf_op jit(solution)/shard_map/reshape | solution.py:31
  33.6 2.2 %fusion.36 = f32[1224,128]{1,0:T(8,128)S(1)} fusion(f32[1224,128]{1,0:T(8,128)} %reshape.101, f32[128,128]{1,0:T(8,128)S(1)} %bitcast.47), kind=kOutput, calls=%fused_computation.99 | convolution fusion | flops 240648192 | bytes 1318912 | tf_op jit(solution)/shard_map/dot_general | solution.py:33
  35.8 2.0 %fusion.37 = f32[1224,128]{1,0:T(8,128)} fusion(f32[1224,128]{1,0:T(8,128)S(1)} %fusion.36, f32[128,128]{1,0:T(8,128)S(1)} %bitcast.48), kind=kOutput, calls=%fused_computation.100 | convolution fusion | flops 240648192 | bytes 1318912 | tf_op jit(solution)/shard_map/dot_general | solution.py:33
  37.7 2.0 %reshape.102 = f32[2,18,34,128]{3,2,1,0:T(8,128)} reshape(f32[1224,128]{1,0:T(8,128)} %fusion.37) | data formatting | bytes 1253376 | tf_op jit(solution)/shard_map/reshape | solution.py:34
  40.0 0.8 copy-done.13
  41.4 0.6 fusion.38
  42.0 0.6 fusion.39
  43.2 3.6 %collective-permute-start.8 = (f32[2,2,32,128]{3,2,1,0:T(8,128)S(1)}, f32[2,2,32,128]{3,2,1,0:T(8,128)S(1)}, u32[]{:S(2)}, u32[]{:S(2)}) collective-permute-start(f32[2,2,32,128]{3,2,1,0:T(8,128)S(1)} %get-tuple-element.31), channel_id=1, source_target_pairs={{0,4},{4,8},{8,12},{12,16},{16,20},{20,24},{24,28},{1,5},{5,9},{9,... | collective-permute-start | bytes 196616 | tf_op jit(solution)/shard_map/ppermute | solution.py:15
  46.8 1.9 %collective-permute-start.9 = (f32[2,2,32,128]{3,2,1,0:T(8,128)S(1)}, f32[2,2,32,128]{3,2,1,0:T(8,128)S(1)}, u32[]{:S(2)}, u32[]{:S(2)}) collective-permute-start(f32[2,2,32,128]{3,2,1,0:T(8,128)S(1)} %get-tuple-element.32), channel_id=1, source_target_pairs={{4,0},{8,4},{12,8},{16,12},{20,16},{24,20},{28,24},{5,1},{9,5},{13... | collective-permute-start | bytes 196616 | tf_op jit(solution)/shard_map/ppermute | solution.py:18
  48.7 3.6 %collective-permute-done.9 = f32[2,2,32,128]{3,2,1,0:T(8,128)S(1)} collective-permute-done((f32[2,2,32,128]{3,2,1,0:T(8,128)S(1)}, f32[2,2,32,128]{3,2,1,0:T(8,128)S(1)}, u32[]{:S(2)}, u32[]{:S(2)}) %collective-permute-start.9) | collective-permute-done | bytes 65568 | tf_op jit(solution)/shard_map/ppermute | solution.py:18
  52.4 4.6 %collective-permute-start.10 = (f32[2,20,2,128]{3,2,1,0:T(2,128)S(1)}, f32[2,20,2,128]{3,2,1,0:T(2,128)S(1)}, u32[]{:S(2)}, u32[]{:S(2)}) collective-permute-start(f32[2,20,2,128]{3,2,1,0:T(2,128)S(1)} %get-tuple-element.25), channel_id=1, source_target_pairs={{0,1},{1,2},{2,3},{4,5},{5,6},{6,7},{8,9},{9,10},{10,11},{12,13},{... | collective-permute-start | bytes 122888 | tf_op jit(solution)/shard_map/ppermute | solution.py:15
  57.0 1.6 %collective-permute-start.11 = (f32[2,20,2,128]{3,2,1,0:T(2,128)S(1)}, f32[2,20,2,128]{3,2,1,0:T(2,128)S(1)}, u32[]{:S(2)}, u32[]{:S(2)}) collective-permute-start(f32[2,20,2,128]{3,2,1,0:T(2,128)S(1)} %get-tuple-element.26), channel_id=1, source_target_pairs={{1,0},{2,1},{3,2},{5,4},{6,5},{7,6},{9,8},{10,9},{11,10},{13,12},{... | collective-permute-start | bytes 122888 | tf_op jit(solution)/shard_map/ppermute | solution.py:18
  58.6 3.3 %collective-permute-done.11 = f32[2,20,2,128]{3,2,1,0:T(2,128)S(1)} collective-permute-done((f32[2,20,2,128]{3,2,1,0:T(2,128)S(1)}, f32[2,20,2,128]{3,2,1,0:T(2,128)S(1)}, u32[]{:S(2)}, u32[]{:S(2)}) %collective-permute-start.11) | collective-permute-done | bytes 40992 | tf_op jit(solution)/shard_map/ppermute | solution.py:18
  62.0 0.9 slice.334
  63.2 2.0 %reshape.105 = f32[1224,128]{1,0:T(8,128)} reshape(f32[2,18,34,128]{3,2,1,0:T(8,128)} %slice.334) | data formatting | bytes 1253376 | tf_op jit(solution)/shard_map/reshape | solution.py:31
  65.2 2.2 %fusion.40 = f32[1224,128]{1,0:T(8,128)S(1)} fusion(f32[1224,128]{1,0:T(8,128)} %reshape.105, f32[128,128]{1,0:T(8,128)S(1)} %bitcast.51), kind=kOutput, calls=%fused_computation.103 | convolution fusion | flops 240648192 | bytes 1318912 | tf_op jit(solution)/shard_map/dot_general | solution.py:33
  67.4 2.0 %fusion.41 = f32[1224,128]{1,0:T(8,128)} fusion(f32[1224,128]{1,0:T(8,128)S(1)} %fusion.40, f32[128,128]{1,0:T(8,128)S(1)} %bitcast.52), kind=kOutput, calls=%fused_computation.104 | convolution fusion | flops 240648192 | bytes 1318912 | tf_op jit(solution)/shard_map/dot_general | solution.py:33
  69.4 2.0 %reshape.106 = f32[2,18,34,128]{3,2,1,0:T(8,128)} reshape(f32[1224,128]{1,0:T(8,128)} %fusion.41) | data formatting | bytes 1253376 | tf_op jit(solution)/shard_map/reshape | solution.py:34
  71.4 1.5 %fusion.11 = f32[2,18,34,128]{3,2,1,0:T(8,128)S(1)} fusion(f32[2,18,34,128]{3,2,1,0:T(8,128)} %reshape.106, f32[2,19,35,128]{3,2,1,0:T(8,128)S(1)} %get-tuple-element.14, f32[2,19,35,128]{3,2,1,0:T(8,128)S(1)} %get-tuple-element.13, pred[18,34]{1,0:T(8,128)(4,1)S(1)} %broadcast_and_fusion, f32[2,20,36,128]{3,2,1,0:T(8,128)S(1)} %pad_maximum_fusion.1), kind=kLoop, calls=%fused_computation.30 | loop fusion | flops 1096704 | bytes 4387428 | tf_op jit(solution)/shard_map/jit(_where)/select_n | solution.py:71
  73.0 0.9 copy-done.5
  74.4 0.6 fusion.42
  75.0 0.6 fusion.43
  75.9 3.4 %collective-permute-start.12 = (f32[2,2,32,128]{3,2,1,0:T(8,128)S(1)}, f32[2,2,32,128]{3,2,1,0:T(8,128)S(1)}, u32[]{:S(2)}, u32[]{:S(2)}) collective-permute-start(f32[2,2,32,128]{3,2,1,0:T(8,128)S(1)} %get-tuple-element.29), channel_id=1, source_target_pairs={{0,4},{4,8},{8,12},{12,16},{16,20},{20,24},{24,28},{1,5},{5,9},{9,... | collective-permute-start | bytes 196616 | tf_op jit(solution)/shard_map/ppermute | solution.py:15
  79.3 1.9 %collective-permute-start.13 = (f32[2,2,32,128]{3,2,1,0:T(8,128)S(1)}, f32[2,2,32,128]{3,2,1,0:T(8,128)S(1)}, u32[]{:S(2)}, u32[]{:S(2)}) collective-permute-start(f32[2,2,32,128]{3,2,1,0:T(8,128)S(1)} %get-tuple-element.30), channel_id=1, source_target_pairs={{4,0},{8,4},{12,8},{16,12},{20,16},{24,20},{28,24},{5,1},{9,5},{13... | collective-permute-start | bytes 196616 | tf_op jit(solution)/shard_map/ppermute | solution.py:18
  81.2 3.6 %collective-permute-done.13 = f32[2,2,32,128]{3,2,1,0:T(8,128)S(1)} collective-permute-done((f32[2,2,32,128]{3,2,1,0:T(8,128)S(1)}, f32[2,2,32,128]{3,2,1,0:T(8,128)S(1)}, u32[]{:S(2)}, u32[]{:S(2)}) %collective-permute-start.13) | collective-permute-done | bytes 65568 | tf_op jit(solution)/shard_map/ppermute | solution.py:18
  84.9 2.5 %collective-permute-start.14 = (f32[2,20,2,128]{3,2,1,0:T(2,128)S(1)}, f32[2,20,2,128]{3,2,1,0:T(2,128)S(1)}, u32[]{:S(2)}, u32[]{:S(2)}) collective-permute-start(f32[2,20,2,128]{3,2,1,0:T(2,128)S(1)} %get-tuple-element.23), channel_id=1, source_target_pairs={{0,1},{1,2},{2,3},{4,5},{5,6},{6,7},{8,9},{9,10},{10,11},{12,13},{... | collective-permute-start | bytes 122888 | tf_op jit(solution)/shard_map/ppermute | solution.py:15
  87.5 1.3 %collective-permute-start.15 = (f32[2,20,2,128]{3,2,1,0:T(2,128)S(1)}, f32[2,20,2,128]{3,2,1,0:T(2,128)S(1)}, u32[]{:S(2)}, u32[]{:S(2)}) collective-permute-start(f32[2,20,2,128]{3,2,1,0:T(2,128)S(1)} %get-tuple-element.24), channel_id=1, source_target_pairs={{1,0},{2,1},{3,2},{5,4},{6,5},{7,6},{9,8},{10,9},{11,10},{13,12},{... | collective-permute-start | bytes 122888 | tf_op jit(solution)/shard_map/ppermute | solution.py:18
  88.8 3.4 %collective-permute-done.15 = f32[2,20,2,128]{3,2,1,0:T(2,128)S(1)} collective-permute-done((f32[2,20,2,128]{3,2,1,0:T(2,128)S(1)}, f32[2,20,2,128]{3,2,1,0:T(2,128)S(1)}, u32[]{:S(2)}, u32[]{:S(2)}) %collective-permute-start.15) | collective-permute-done | bytes 40992 | tf_op jit(solution)/shard_map/ppermute | solution.py:18
  92.7 0.9 reshape.109
  93.6 2.2 %fusion.44 = f32[1224,128]{1,0:T(8,128)S(1)} fusion(f32[1224,128]{1,0:T(8,128)} %reshape.109, f32[128,128]{1,0:T(8,128)S(1)} %bitcast.55), kind=kOutput, calls=%fused_computation.107 | convolution fusion | flops 240648192 | bytes 1318912 | tf_op jit(solution)/shard_map/dot_general | solution.py:33
  95.8 2.0 %fusion.45 = f32[1224,128]{1,0:T(8,128)} fusion(f32[1224,128]{1,0:T(8,128)S(1)} %fusion.44, f32[128,128]{1,0:T(8,128)S(1)} %bitcast.56), kind=kOutput, calls=%fused_computation.108 | convolution fusion | flops 240648192 | bytes 1318912 | tf_op jit(solution)/shard_map/dot_general | solution.py:33
  97.7 1.1 %reshape.110 = f32[2,18,34,128]{3,2,1,0:T(8,128)S(1)} reshape(f32[1224,128]{1,0:T(8,128)} %fusion.45) | data formatting | bytes 1253376 | tf_op jit(solution)/shard_map/reshape | solution.py:34
  100.4 0.6 fusion.46
  101.0 0.6 fusion.47
  101.6 1.1 %fusion.20 = f32[2,16,32,128]{3,2,1,0:T(8,128)} fusion(f32[2,16,32,128]{3,2,1,0:T(8,128)S(1)} %bitcast.60, f32[2,17,33,128]{3,2,1,0:T(8,128)S(1)} %get-tuple-element.18, f32[2,17,33,128]{3,2,1,0:T(8,128)S(1)} %get-tuple-element.17, f32[2,18,34,128]{3,2,1,0:T(8,128)S(1)} %fusion.6), kind=kLoop, calls=%fused_computation.56 | loop fusion | flops 786432 | bytes 3670016 | tf_op jit(solution)/shard_map/sub | solution.py:73
  (78 shorter events, 5.9 us)
Async XLA Ops:
  0.0 14.3 %copy-start = (f32[41]{0:T(128)S(1)}, f32[41]{0:T(128)}, u32[]{:S(2)}) copy-start(f32[41]{0:T(128)} %param.5) | copy-start | bytes 496
  0.8 15.3 %collective-permute-start.5 = (bf16[3,2,32,128]{3,2,1,0:T(8,128)(2,1)S(1)}, bf16[3,2,32,128]{3,2,1,0:T(8,128)(2,1)S(1)}, u32[]{:S(2)}, u32[]{:S(2)}) collective-permute-start(bf16[3,2,32,128]{3,2,1,0:T(8,128)(2,1)S(1)} %get-tuple-element.37), channel_id=1, source_target_pairs={{4,0},{8,4},{12,8},{16,12},{20,16},{24,20},{28,24},{5,1},{9,5},{13... | collective-permute-start | bytes 147464 | tf_op jit(solution)/shard_map/ppermute | solution.py:18
  2.8 13.2 %collective-permute-start.4 = (bf16[3,2,32,128]{3,2,1,0:T(8,128)(2,1)S(1)}, bf16[3,2,32,128]{3,2,1,0:T(8,128)(2,1)S(1)}, u32[]{:S(2)}, u32[]{:S(2)}) collective-permute-start(bf16[3,2,32,128]{3,2,1,0:T(8,128)(2,1)S(1)} %get-tuple-element.38), channel_id=1, source_target_pairs={{0,4},{4,8},{8,12},{12,16},{16,20},{20,24},{24,28},{1,5},{5,9},{9,... | collective-permute-start | bytes 147464 | tf_op jit(solution)/shard_map/ppermute | solution.py:15
  8.3 12.5 %collective-permute-start.1 = (f32[2,2,32,128]{3,2,1,0:T(8,128)S(1)}, f32[2,2,32,128]{3,2,1,0:T(8,128)S(1)}, u32[]{:S(2)}, u32[]{:S(2)}) collective-permute-start(f32[2,2,32,128]{3,2,1,0:T(8,128)S(1)} %get-tuple-element.33), channel_id=1, source_target_pairs={{4,0},{8,4},{12,8},{16,12},{20,16},{24,20},{28,24},{5,1},{9,5},{13... | collective-permute-start | bytes 196616 | tf_op jit(solution)/shard_map/ppermute | solution.py:18
  10.2 10.5 %collective-permute-start = (f32[2,2,32,128]{3,2,1,0:T(8,128)S(1)}, f32[2,2,32,128]{3,2,1,0:T(8,128)S(1)}, u32[]{:S(2)}, u32[]{:S(2)}) collective-permute-start(f32[2,2,32,128]{3,2,1,0:T(8,128)S(1)} %get-tuple-element.34), channel_id=1, source_target_pairs={{0,4},{4,8},{8,12},{12,16},{16,20},{20,24},{24,28},{1,5},{5,9},{9,... | collective-permute-start | bytes 196616 | tf_op jit(solution)/shard_map/ppermute | solution.py:15
  14.3 1.8 %copy-start.15 = (bf16[3,16,32,128]{3,2,1,0:T(8,128)(2,1)S(1)}, bf16[3,16,32,128]{3,2,1,0:T(8,128)(2,1)}, u32[]{:S(2)}) copy-start(bf16[3,16,32,128]{3,2,1,0:T(8,128)(2,1)} %param.4) | copy-start | bytes 1179652
  14.3 6.3 %copy-start.14 = (f32[2,16,32,128]{3,2,1,0:T(8,128)S(1)}, f32[2,16,32,128]{3,2,1,0:T(8,128)}, u32[]{:S(2)}) copy-start(f32[2,16,32,128]{3,2,1,0:T(8,128)} %param.3) | copy-start | bytes 1572868
  16.2 9.9 %collective-permute-start.6 = (bf16[3,20,2,128]{3,2,1,0:T(2,128)(2,1)S(1)}, bf16[3,20,2,128]{3,2,1,0:T(2,128)(2,1)S(1)}, u32[]{:S(2)}, u32[]{:S(2)}) collective-permute-start(bf16[3,20,2,128]{3,2,1,0:T(2,128)(2,1)S(1)} %get-tuple-element.35), channel_id=1, source_target_pairs={{0,1},{1,2},{2,3},{4,5},{5,6},{6,7},{8,9},{9,10},{10,11},{12,13},{... | collective-permute-start | bytes 92168 | tf_op jit(solution)/shard_map/ppermute | solution.py:15
  19.3 6.8 %collective-permute-start.7 = (bf16[3,20,2,128]{3,2,1,0:T(2,128)(2,1)S(1)}, bf16[3,20,2,128]{3,2,1,0:T(2,128)(2,1)S(1)}, u32[]{:S(2)}, u32[]{:S(2)}) collective-permute-start(bf16[3,20,2,128]{3,2,1,0:T(2,128)(2,1)S(1)} %get-tuple-element.36), channel_id=1, source_target_pairs={{1,0},{2,1},{3,2},{5,4},{6,5},{7,6},{9,8},{10,9},{11,10},{13,12},{... | collective-permute-start | bytes 92168 | tf_op jit(solution)/shard_map/ppermute | solution.py:18
  20.8 5.8 %collective-permute-start.2 = (f32[2,20,2,128]{3,2,1,0:T(2,128)S(1)}, f32[2,20,2,128]{3,2,1,0:T(2,128)S(1)}, u32[]{:S(2)}, u32[]{:S(2)}) collective-permute-start(f32[2,20,2,128]{3,2,1,0:T(2,128)S(1)} %get-tuple-element.27), channel_id=1, source_target_pairs={{0,1},{1,2},{2,3},{4,5},{5,6},{6,7},{8,9},{9,10},{10,11},{12,13},{... | collective-permute-start | bytes 122888 | tf_op jit(solution)/shard_map/ppermute | solution.py:15
  24.8 5.7 %collective-permute-start.3 = (f32[2,20,2,128]{3,2,1,0:T(2,128)S(1)}, f32[2,20,2,128]{3,2,1,0:T(2,128)S(1)}, u32[]{:S(2)}, u32[]{:S(2)}) collective-permute-start(f32[2,20,2,128]{3,2,1,0:T(2,128)S(1)} %get-tuple-element.28), channel_id=1, source_target_pairs={{1,0},{2,1},{3,2},{5,4},{6,5},{7,6},{9,8},{10,9},{11,10},{13,12},{... | collective-permute-start | bytes 122888 | tf_op jit(solution)/shard_map/ppermute | solution.py:18
  26.4 13.3 %copy-start.1 = (f32[19,35,128]{2,1,0:T(8,128)}, f32[19,35,128]{2,1,0:T(8,128)S(1)}, u32[]{:S(2)}) copy-start(f32[19,35,128]{2,1,0:T(8,128)S(1)} %get-tuple-element.10) | copy-start | bytes 1021444
  26.5 16.0 %copy-start.4 = (f32[17,33,128]{2,1,0:T(8,128)}, f32[17,33,128]{2,1,0:T(8,128)S(1)}, u32[]{:S(2)}) copy-start(f32[17,33,128]{2,1,0:T(8,128)S(1)} %get-tuple-element.5) | copy-start | bytes 861700
  26.6 16.0 %copy-start.7 = (f32[17,33,128]{2,1,0:T(8,128)}, f32[17,33,128]{2,1,0:T(8,128)S(1)}, u32[]{:S(2)}) copy-start(f32[17,33,128]{2,1,0:T(8,128)S(1)} %get-tuple-element.6) | copy-start | bytes 861700
  26.6 16.0 %copy-start.10 = (f32[17,33,128]{2,1,0:T(8,128)}, f32[17,33,128]{2,1,0:T(8,128)S(1)}, u32[]{:S(2)}) copy-start(f32[17,33,128]{2,1,0:T(8,128)S(1)} %get-tuple-element.7) | copy-start | bytes 861700
  39.8 1.1 %copy-start.13 = (f32[2,18,34,128]{3,2,1,0:T(8,128)S(1)}, f32[2,18,34,128]{3,2,1,0:T(8,128)}, u32[]{:S(2)}) copy-start(f32[2,18,34,128]{3,2,1,0:T(8,128)} %reshape.102) | copy-start | bytes 1880068
  43.2 5.5 %collective-permute-start.8 = (f32[2,2,32,128]{3,2,1,0:T(8,128)S(1)}, f32[2,2,32,128]{3,2,1,0:T(8,128)S(1)}, u32[]{:S(2)}, u32[]{:S(2)}) collective-permute-start(f32[2,2,32,128]{3,2,1,0:T(8,128)S(1)} %get-tuple-element.31), channel_id=1, source_target_pairs={{0,4},{4,8},{8,12},{12,16},{16,20},{20,24},{24,28},{1,5},{5,9},{9,... | collective-permute-start | bytes 196616 | tf_op jit(solution)/shard_map/ppermute | solution.py:15
  46.8 5.6 %collective-permute-start.9 = (f32[2,2,32,128]{3,2,1,0:T(8,128)S(1)}, f32[2,2,32,128]{3,2,1,0:T(8,128)S(1)}, u32[]{:S(2)}, u32[]{:S(2)}) collective-permute-start(f32[2,2,32,128]{3,2,1,0:T(8,128)S(1)} %get-tuple-element.32), channel_id=1, source_target_pairs={{4,0},{8,4},{12,8},{16,12},{20,16},{24,20},{28,24},{5,1},{9,5},{13... | collective-permute-start | bytes 196616 | tf_op jit(solution)/shard_map/ppermute | solution.py:18
  52.4 6.2 %collective-permute-start.10 = (f32[2,20,2,128]{3,2,1,0:T(2,128)S(1)}, f32[2,20,2,128]{3,2,1,0:T(2,128)S(1)}, u32[]{:S(2)}, u32[]{:S(2)}) collective-permute-start(f32[2,20,2,128]{3,2,1,0:T(2,128)S(1)} %get-tuple-element.25), channel_id=1, source_target_pairs={{0,1},{1,2},{2,3},{4,5},{5,6},{6,7},{8,9},{9,10},{10,11},{12,13},{... | collective-permute-start | bytes 122888 | tf_op jit(solution)/shard_map/ppermute | solution.py:15
  57.0 5.9 %copy-start.2 = (f32[19,35,128]{2,1,0:T(8,128)S(1)}, f32[19,35,128]{2,1,0:T(8,128)}, u32[]{:S(2)}) copy-start(f32[19,35,128]{2,1,0:T(8,128)} %copy-done.1) | copy-start | bytes 1021444
  57.0 4.9 %collective-permute-start.11 = (f32[2,20,2,128]{3,2,1,0:T(2,128)S(1)}, f32[2,20,2,128]{3,2,1,0:T(2,128)S(1)}, u32[]{:S(2)}, u32[]{:S(2)}) collective-permute-start(f32[2,20,2,128]{3,2,1,0:T(2,128)S(1)} %get-tuple-element.26), channel_id=1, source_target_pairs={{1,0},{2,1},{3,2},{5,4},{6,5},{7,6},{9,8},{10,9},{11,10},{13,12},{... | collective-permute-start | bytes 122888 | tf_op jit(solution)/shard_map/ppermute | solution.py:18
  72.9 1.0 copy-start.5
  73.0 1.1 %copy-start.8 = (f32[17,33,128]{2,1,0:T(8,128)S(1)}, f32[17,33,128]{2,1,0:T(8,128)}, u32[]{:S(2)}) copy-start(f32[17,33,128]{2,1,0:T(8,128)} %copy-done.7) | copy-start | bytes 861700
  73.0 1.2 %copy-start.11 = (f32[17,33,128]{2,1,0:T(8,128)S(1)}, f32[17,33,128]{2,1,0:T(8,128)}, u32[]{:S(2)}) copy-start(f32[17,33,128]{2,1,0:T(8,128)} %copy-done.10) | copy-start | bytes 861700
  75.8 16.5 %copy-start.3 = (f32[19,35,128]{2,1,0:T(8,128)S(1)}, f32[19,35,128]{2,1,0:T(8,128)}, u32[]{:S(2)}) copy-start(f32[19,35,128]{2,1,0:T(8,128)} %copy-done.1) | copy-start | bytes 1021444
  75.9 5.4 %collective-permute-start.12 = (f32[2,2,32,128]{3,2,1,0:T(8,128)S(1)}, f32[2,2,32,128]{3,2,1,0:T(8,128)S(1)}, u32[]{:S(2)}, u32[]{:S(2)}) collective-permute-start(f32[2,2,32,128]{3,2,1,0:T(8,128)S(1)} %get-tuple-element.29), channel_id=1, source_target_pairs={{0,4},{4,8},{8,12},{12,16},{16,20},{20,24},{24,28},{1,5},{5,9},{9,... | collective-permute-start | bytes 196616 | tf_op jit(solution)/shard_map/ppermute | solution.py:15
  79.3 5.6 %collective-permute-start.13 = (f32[2,2,32,128]{3,2,1,0:T(8,128)S(1)}, f32[2,2,32,128]{3,2,1,0:T(8,128)S(1)}, u32[]{:S(2)}, u32[]{:S(2)}) collective-permute-start(f32[2,2,32,128]{3,2,1,0:T(8,128)S(1)} %get-tuple-element.30), channel_id=1, source_target_pairs={{4,0},{8,4},{12,8},{16,12},{20,16},{24,20},{28,24},{5,1},{9,5},{13... | collective-permute-start | bytes 196616 | tf_op jit(solution)/shard_map/ppermute | solution.py:18
  84.9 3.9 %collective-permute-start.14 = (f32[2,20,2,128]{3,2,1,0:T(2,128)S(1)}, f32[2,20,2,128]{3,2,1,0:T(2,128)S(1)}, u32[]{:S(2)}, u32[]{:S(2)}) collective-permute-start(f32[2,20,2,128]{3,2,1,0:T(2,128)S(1)} %get-tuple-element.23), channel_id=1, source_target_pairs={{0,1},{1,2},{2,3},{4,5},{5,6},{6,7},{8,9},{9,10},{10,11},{12,13},{... | collective-permute-start | bytes 122888 | tf_op jit(solution)/shard_map/ppermute | solution.py:15
  87.5 4.7 %collective-permute-start.15 = (f32[2,20,2,128]{3,2,1,0:T(2,128)S(1)}, f32[2,20,2,128]{3,2,1,0:T(2,128)S(1)}, u32[]{:S(2)}, u32[]{:S(2)}) collective-permute-start(f32[2,20,2,128]{3,2,1,0:T(2,128)S(1)} %get-tuple-element.24), channel_id=1, source_target_pairs={{1,0},{2,1},{3,2},{5,4},{6,5},{7,6},{9,8},{10,9},{11,10},{13,12},{... | collective-permute-start | bytes 122888 | tf_op jit(solution)/shard_map/ppermute | solution.py:18
  98.9 1.0 copy-start.6
  98.9 1.1 %copy-start.9 = (f32[17,33,128]{2,1,0:T(8,128)S(1)}, f32[17,33,128]{2,1,0:T(8,128)}, u32[]{:S(2)}) copy-start(f32[17,33,128]{2,1,0:T(8,128)} %copy-done.7) | copy-start | bytes 861700
  98.9 1.2 %copy-start.12 = (f32[17,33,128]{2,1,0:T(8,128)S(1)}, f32[17,33,128]{2,1,0:T(8,128)}, u32[]{:S(2)}) copy-start(f32[17,33,128]{2,1,0:T(8,128)} %copy-done.10) | copy-start | bytes 861700
where the time goes:
time: 104 us; the launch traced here: 103 us
  starting transfers between devices  42.6 us (41%)
  waiting for transfers between devices  17.9 us (17%)
  matrix products  17.6 us (17%)
  local copies, waits for them, and re-layouts  17 us (16%)
  other arithmetic  6.8 us (7%)
    ppermute x8, starting transfers between devices, with_halo(): lax.ppermute(lax.slice_in_dim(block, block.shape[dim] - width, None, axis...  29.4 us
    ppermute x8, waiting for transfers between devices, with_halo(): lax.ppermute(lax.slice_in_dim(block, 0, width, axis=dim), axis, backward)  17.9 us
    dot_general x12, matrix products, apply_data(): trace_rows = jnp.dot(trace_rows, matrix, precision=lax.Precision.HIGHEST)  16 us
    ppermute x8, starting transfers between devices, with_halo(): lax.ppermute(lax.slice_in_dim(block, 0, width, axis=dim), axis, backward)  13.2 us
    reshape x3, local copies, waits for them, and re-layouts, apply_data(): return trace_rows.reshape(shape)  5.15 us
    reshape x3, local copies, waits for them, and re-layouts, apply_data(): trace_rows = volume.reshape(-1, shape[-1])  4.85 us
    unnamed x36, local copies, waits for them, and re-layouts  2.87 us
    select_n x3, other arithmetic, per_device(): first_pass = jnp.where(inside, first_pass, jnp.float32(0.0))  2.38 us
  transfers between devices with their start and end apart: 16, of which 5 were waited for; matrix products, arithmetic and copies ran while one was open for 4% of the time, Pallas kernels for 0%

commit v1 on v0

v1 whole, which is shorter than its diff:
```python
import functools

import jax
import jax.numpy as jnp
from jax import lax
from jax.experimental import pallas as pl
from jax.experimental.pallas import tpu as pltpu
from jax.sharding import PartitionSpec as P

STEPS = 6
WIDTH = 2
ROUNDS = STEPS // WIDTH
DAMPING = 0.25
VECTORS = 2
PLANES = VECTORS + 3
LANES = 128
SUB = 8
WAYS = ((-1, 0), (1, 0), (0, -1), (0, 1), (-1, -1), (-1, 1), (1, -1), (1, 1))


def kernel(probes, diffusion, wavelet, out, *scratch):
    H = WIDTH
    nv, I, J, S = probes.shape
    C = J + SUB
    R = I + 2 * H
    at = 0

    def take(count):
        nonlocal at
        at += count
        return scratch[at - count:at]

    xs = take(ROUNDS)
    ys = take(ROUNDS * (H - 1))
    east_out = take(ROUNDS)
    west_out = take(ROUNDS)
    east_in = take(ROUNDS)
    west_in = take(ROUNDS)
    raw, smooth, mat, load_sem, send_sem, recv_sem = take(6)

    me_in = lax.axis_index("inline")
    me_x = lax.axis_index("xline")
    n_in = lax.axis_size("inline")
    n_x = lax.axis_size("xline")
    has = {
        (-1, 0): me_in > 0,
        (1, 0): me_in < n_in - 1,
        (0, -1): me_x > 0,
        (0, 1): me_x < n_x - 1,
    }
    for di, dx in WAYS[4:]:
        has[(di, dx)] = jnp.logical_and(has[(di, 0)], has[(0, dx)])

    def device(way):
        return {"inline": me_in + way[0], "xline": me_x + way[1]}

    loads = [
        pltpu.make_async_copy(diffusion, raw, load_sem.at[0]),
        pltpu.make_async_copy(probes.at[0], xs[0].at[1, H:H + I, 0:J], load_sem.at[1]),
        pltpu.make_async_copy(probes.at[1], xs[0].at[0, H:H + I, 0:J], load_sem.at[2]),
    ]
    for load in loads:
        load.start()

    barrier = pltpu.get_barrier_semaphore()
    for way in WAYS:
        @pl.when(has[way])
        def _(way=way):
            pl.semaphore_signal(
                barrier, inc=1, device_id=device(way), device_id_type=pl.DeviceIdType.MESH
            )

    for r in range(ROUNDS):
        for side, rows in (((-1, 0), slice(0, H)), ((1, 0), slice(H + I, R))):
            @pl.when(jnp.logical_not(has[side]))
            def _(r=r, rows=rows):
                planes = xs[r].shape[0]
                xs[r][:, rows, 0:J] = jnp.zeros((planes, H, J, S), jnp.float32)
                east_in[r][:, rows] = jnp.zeros((planes, H, H, S), jnp.float32)
                west_in[r][:, rows] = jnp.zeros((planes, H, H, S), jnp.float32)
        for side, buffer in (((0, 1), east_in[r]), ((0, -1), west_in[r])):
            @pl.when(jnp.logical_not(has[side]))
            def _(buffer=buffer):
                buffer[...] = jnp.zeros(buffer.shape, jnp.float32)

    neighbours = (
        (1 + has[(-1, 0)].astype(jnp.int32) + has[(1, 0)].astype(jnp.int32))
        * (1 + has[(0, -1)].astype(jnp.int32) + has[(0, 1)].astype(jnp.int32))
        - 1
    )

    def copies(r, group, planes):
        x = xs[r]
        p = slice(*planes)
        low, high = slice(0, H), slice(H + I, R)
        middle = slice(H, H + I)
        ends = {
            (-1, 0): (x.at[p, H:2 * H, 0:J], x.at[p, high, 0:J]),
            (1, 0): (x.at[p, I:I + H, 0:J], x.at[p, low, 0:J]),
            (0, -1): (west_out[r].at[p], east_in[r].at[p, middle]),
            (0, 1): (east_out[r].at[p], west_in[r].at[p, middle]),
            (-1, -1): (west_out[r].at[p, 0:H], east_in[r].at[p, high]),
            (-1, 1): (east_out[r].at[p, 0:H], west_in[r].at[p, high]),
            (1, -1): (west_out[r].at[p, I - H:I], east_in[r].at[p, low]),
            (1, 1): (east_out[r].at[p, I - H:I], west_in[r].at[p, low]),
        }
        return {
            way: pltpu.make_async_remote_copy(
                src_ref=ends[way][0],
                dst_ref=ends[way][1],
                send_sem=send_sem.at[r, group, k],
                recv_sem=recv_sem.at[r, group, k],
                device_id=device(way),
                device_id_type=pl.DeviceIdType.MESH,
            )
            for k, way in enumerate(WAYS)
        }

    def planes_of(r, group):
        if group == 1:
            return (0, 1)
        return (1, PLANES) if r == 0 else (1, 2)

    def pack(r, planes):
        for p in range(*planes):
            def body(i, carry, p=p):
                west_out[r][p, i] = xs[r][p, H + i, 0:H]
                east_out[r][p, i] = xs[r][p, H + i, J - H:J]
                return carry
            lax.fori_loop(0, I, body, 0)

    def send(r, group):
        made = copies(r, group, planes_of(r, group))
        for way in WAYS:
            @pl.when(has[way])
            def _(way=way):
                made[way].start()

    def receive(r, group):
        planes = planes_of(r, group)
        made = copies(r, group, planes)
        for way in WAYS:
            @pl.when(has[(-way[0], -way[1])])
            def _(way=way):
                made[way].wait_recv()
        for p in range(*planes):
            def body(i, carry, p=p):
                xs[r][p, i, J:J + H] = east_in[r][p, i]
                xs[r][p, i, C - H:C] = west_in[r][p, i]
                return carry
            lax.fori_loop(0, R, body, 0)

    def step(src, dst, plane, low, high, store):
        rows = (high - low) * C
        block = src[plane, low:high].reshape(rows, S)
        top = block.astype(jnp.bfloat16)
        rest = (block - top.astype(jnp.float32)).astype(jnp.bfloat16)
        both = jnp.dot(
            jnp.concatenate([top, rest], axis=1), mat[...], preferred_element_type=jnp.float32
        )
        smooth[low:high] = (both[:, :S] + both[:, S:]).reshape(high - low, C, S)
        tensor = xs[0]

        def flux(i, here):
            below = src[plane, i + 1]
            a, b, c = tensor[VECTORS, i], tensor[VECTORS + 1, i], tensor[VECTORS + 2, i]
            step_in = below - here
            step_x = pltpu.roll(here, C - 1, axis=0) - here
            return below, a * step_in + b * step_x, b * step_in + c * step_x

        def body(n, carry):
            here, above = carry
            for k in range(2):
                i = low + 2 * n + k
                below, flux_in, flux_x = flux(i, here)
                fresh = smooth[i] - ((above - flux_in) + (pltpu.roll(flux_x, 1, axis=0) - flux_x))
                store(dst, i, fresh)
                here, above = below, flux_in
            return here, above

        here, above, _ = flux(low - 1, src[plane, low - 1])
        lax.fori_loop(0, (high - low) // 2, body, (here, above))

    loads[0].wait()
    for q in range(3):
        xs[0][VECTORS + q, H:H + I, 0:J] = raw[q].astype(jnp.float32) * DAMPING
    loads[1].wait()
    pack(0, planes_of(0, 0))
    pl.semaphore_wait(barrier, neighbours)
    send(0, 0)
    loads[2].wait()
    pack(0, planes_of(0, 1))
    send(0, 1)

    row = lax.broadcasted_iota(jnp.int32, (S, S), 0)
    col = lax.broadcasted_iota(jnp.int32, (S, S), 1)
    taps = wavelet.shape[0]
    offset = col - row + taps // 2
    band = jnp.zeros((S, S), jnp.float32)
    for k in range(taps):
        band = jnp.where(offset == k, wavelet[k], band)
    gram = lax.dot_general(
        band, band, (((1,), (1,)), ((), ())),
        precision=lax.Precision.HIGHEST, preferred_element_type=jnp.float32,
    )
    whole = jnp.where(row == col, jnp.float32(1.0), jnp.float32(0.0)) - DAMPING * gram
    top = whole.astype(jnp.bfloat16)
    rest = (whole - top.astype(jnp.float32)).astype(jnp.bfloat16)
    for k in range(2):
        mat[k * S:(k + 1) * S, 0:S] = top
        mat[k * S:(k + 1) * S, S:2 * S] = rest

    for r in range(ROUNDS):
        for group in range(2):
            plane = 1 - group
            receive(r, group)
            src = xs[r]
            for k in range(1, H + 1):
                extra = H - k
                low, high = H - extra, H + I + extra
                last = k == H
                if not last:
                    dst = ys[r * (H - 1) + k - 1]

                    def store(dst, i, value):
                        dst[plane, i] = value
                elif r < ROUNDS - 1:
                    dst = xs[r + 1]

                    def store(dst, i, value):
                        dst[plane, i, 0:J] = value[0:J]
                        west_out[r + 1][plane, i - H] = value[0:H]
                        east_out[r + 1][plane, i - H] = value[J - H:J]
                else:
                    dst = out

                    def store(dst, i, value):
                        dst[group, i - H] = value[0:J]
                step(src, dst, plane, low, high, store)
                if not last:
                    @pl.when(jnp.logical_not(has[(1, 0)]))
                    def _():
                        dst[plane, H + I:high] = jnp.zeros((extra, C, S), jnp.float32)

                    @pl.when(jnp.logical_not(has[(0, 1)]))
                    def _():
                        dst[plane, low:high, J:J + extra] = jnp.zeros((high - low, extra, S), jnp.float32)
                src = dst
            if r < ROUNDS - 1:
                send(r + 1, group)

    for r in range(ROUNDS):
        for group in range(2):
            made = copies(r, group, planes_of(r, group))
            for way in WAYS:
                @pl.when(has[way])
                def _(way=way):
                    made[way].wait_send()


def per_device(probes, diffusion, wavelet):
    nv, I, J, S = probes.shape
    H = WIDTH
    C = J + SUB
    R = I + 2 * H
    f32 = jnp.float32
    planes = [PLANES] + [VECTORS] * (ROUNDS - 1)
    scratch = (
        [pltpu.VMEM((p, R, C, S), f32) for p in planes]
        + [pltpu.VMEM((VECTORS, R, C, S), f32) for _ in range(ROUNDS * (H - 1))]
        + [pltpu.VMEM((p, I, H, S), f32) for p in planes] * 2
        + [pltpu.VMEM((p, R, H, S), f32) for p in planes] * 2
        + [
            pltpu.VMEM(diffusion.shape, diffusion.dtype),
            pltpu.VMEM((R, C, S), f32),
            pltpu.VMEM((2 * S, 2 * S), jnp.bfloat16),
            pltpu.SemaphoreType.DMA((3,)),
            pltpu.SemaphoreType.DMA((ROUNDS, 2, len(WAYS))),
            pltpu.SemaphoreType.DMA((ROUNDS, 2, len(WAYS))),
        ]
    )
    return pl.pallas_call(
        kernel,
        out_shape=jax.ShapeDtypeStruct(probes.shape, f32),
        in_specs=[
            pl.BlockSpec(memory_space=pl.ANY),
            pl.BlockSpec(memory_space=pl.ANY),
            pl.BlockSpec(memory_space=pltpu.SMEM),
        ],
        out_specs=pl.BlockSpec(memory_space=pltpu.VMEM),
        scratch_shapes=scratch,
        compiler_params=pltpu.CompilerParams(
            collective_id=0, has_side_effects=True, vmem_limit_bytes=32 * 1024 * 1024
        ),
        cost_estimate=pl.CostEstimate(flops=STEPS * 2 * 1024 * 256 * 256, bytes_accessed=1500000, transcendentals=0),
    )(probes, diffusion, wavelet)


def solution(mesh):
    return jax.shard_map(
        per_device,
        mesh=mesh,
        in_specs=(P(None, "inline", "xline", None), P(None, "inline", "xline", None), P()),
        out_specs=P(None, "inline", "xline", None),
        check_vma=False,
    )
```

time: 104 us -> 27.7 us (0.27); the launches traced: 103 us -> 27.5 us
  starting transfers between devices: 42.6 us -> 0 us
  Pallas kernels: 0 us -> 24 us
  waiting for transfers between devices: 17.9 us -> 0 us
  matrix products: 17.6 us -> 0 us
  local copies, waits for them, and re-layouts: 17 us -> 3.49 us
  other arithmetic: 6.8 us -> 0 us
    ppermute x16 -> x0, starting transfers between devices: 42.6 us -> none  [the longest x8 29.4 us: with_halo(): lax.ppermute(lax.slice_in_dim(block, block.shape[dim] - width, None, axis...]
    pallas_call x0 -> x1, Pallas kernels: none -> 24 us  [per_device(): pl.pallas_call(kernel, out_shape=jax.ShapeDtypeStruct(probes.shape, f32),...]
    ppermute x16 -> x0, waiting for transfers between devices: 17.9 us -> none  [the longest x8 17.9 us: with_halo(): lax.ppermute(lax.slice_in_dim(block, 0, width, axis=dim), axis, backward)]
    dot_general x13 -> x0, matrix products: 17.6 us -> none  [the longest x12 16 us: apply_data(): trace_rows = jnp.dot(trace_rows, matrix, precision=lax.Precision.HIGHEST)]
    reshape x6 -> x0, local copies, waits for them, and re-layouts: 9.99 us -> none  [the longest x3 5.15 us: apply_data(): return trace_rows.reshape(shape)]
    slice x12 -> x0, local copies, waits for them, and re-layouts: 3.95 us -> none  [the longest x3 1.94 us: per_device(): centre = extended[:, 1:-1, 1:-1]]
    select_n x3 -> x0, other arithmetic: 2.38 us -> none  [per_device(): first_pass = jnp.where(inside, first_pass, jnp.float32(0.0))]
    add x7 -> x0, other arithmetic: 1.65 us -> none  [the longest x6 1.64 us: regularize(): flux_in = tensor[0] * step_in + tensor[1] * step_x]
  transfers between devices with their start and end apart: 16 -> 0, of which waited for: 5 -> 0; matrix products, arithmetic and copies ran while one was open for 4% -> 0% of each run, Pallas kernels for 0% -> 0%
where the time goes in v1:
time: 27.7 us; the launch traced here: 27.5 us
  Pallas kernels  24 us (87%)
  local copies, waits for them, and re-layouts  3.49 us (13%)
    pallas_call x1, Pallas kernels, per_device(): pl.pallas_call(kernel, out_shape=jax.ShapeDtypeStruct(probes.shape, f32),...  24 us
    unnamed x7, local copies, waits for them, and re-layouts  3.49 us

profile of v1, /device:TPU:1, one launch (start us, length us, event | category | flops | bytes accessed | tf_op | source)
XLA Modules:
  0.0 27.5 jit_solution(4513712903517105873)
XLA Ops:
  0.0 0.0 copy-start
  0.0 1.0 %copy-done = f32[2,16,32,128]{3,2,1,0:T(8,128)S(1)} copy-done((f32[2,16,32,128]{3,2,1,0:T(8,128)S(1)}, f32[2,16,32,128]{3,2,1,0:T(8,128)}, u32[]{:S(2)}) %copy-start) | copy-done | bytes 524312
  1.0 0.0 copy-start.1
  1.0 1.0 %copy-done.1 = bf16[3,16,32,128]{3,2,1,0:T(8,128)(2,1)S(1)} copy-done((bf16[3,16,32,128]{3,2,1,0:T(8,128)(2,1)S(1)}, bf16[3,16,32,128]{3,2,1,0:T(8,128)(2,1)}, u32[]{:S(2)}) %copy-start.1) | copy-done | bytes 393240
  2.0 0.0 copy-start.2
  2.0 0.7 %copy-done.2 = f32[41]{0:T(128)S(1)} copy-done((f32[41]{0:T(128)S(1)}, f32[41]{0:T(128)}, u32[]{:S(2)}) %copy-start.2) | copy-done | bytes 188
  2.7 24.0 %shard_map.37 = f32[2,16,32,128]{3,2,1,0:T(8,128)S(1)} custom-call(f32[2,16,32,128]{3,2,1,0:T(8,128)S(1)} %copy-done, bf16[3,16,32,128]{3,2,1,0:T(8,128)(2,1)S(1)} %copy-done.1, f32[41]{0:T(128)S(1)} %copy-done.2), custom_call_target="tpu_custom_call" | custom-call | flops 805306368 | bytes 1500000 | tf_op jit(solution)/shard_map/pallas_call | solution.py:282
  26.7 0.8 %copy.5 = f32[2,16,32,128]{3,2,1,0:T(8,128)} copy(f32[2,16,32,128]{3,2,1,0:T(8,128)S(1)} %shard_map.37) | data formatting | bytes 1048576
Async XLA Ops:
  0.0 1.0 %copy-start = (f32[2,16,32,128]{3,2,1,0:T(8,128)S(1)}, f32[2,16,32,128]{3,2,1,0:T(8,128)}, u32[]{:S(2)}) copy-start(f32[2,16,32,128]{3,2,1,0:T(8,128)} %probes.1) | copy-start | bytes 1572868
  1.0 1.0 %copy-start.1 = (bf16[3,16,32,128]{3,2,1,0:T(8,128)(2,1)S(1)}, bf16[3,16,32,128]{3,2,1,0:T(8,128)(2,1)}, u32[]{:S(2)}) copy-start(bf16[3,16,32,128]{3,2,1,0:T(8,128)(2,1)} %diffusion.1) | copy-start | bytes 1179652
  2.0 0.7 %copy-start.2 = (f32[41]{0:T(128)S(1)}, f32[41]{0:T(128)}, u32[]{:S(2)}) copy-start(f32[41]{0:T(128)} %wavelet.1) | copy-start | bytes 496

commit v2 on v1

v2 whole, which is shorter than its diff:
```python
import functools

import jax
import jax.numpy as jnp
from jax import lax
from jax.experimental import pallas as pl
from jax.experimental.pallas import tpu as pltpu
from jax.sharding import PartitionSpec as P

STEPS = 6
WIDTH = 2
ROUNDS = STEPS // WIDTH
DAMPING = 0.25
VECTORS = 2
PLANES = VECTORS + 3
SUB = 8
TILE = 16
WAYS = ((-1, 0), (1, 0), (0, -1), (0, 1), (-1, -1), (-1, 1), (1, -1), (1, 1))


def kernel(probes, diffusion, wavelet, out, *scratch):
    H = WIDTH
    nv, I, J, S = probes.shape
    C = J + SUB
    R = I + 2 * H
    f32, bf16 = jnp.float32, jnp.bfloat16
    at = 0

    def take(count):
        nonlocal at
        at += count
        return scratch[at - count:at]

    xs = take(ROUNDS)
    ys = take(ROUNDS * (H - 1))
    made_side = (take(1)[0], take(1)[0])
    sent_side = (take(ROUNDS), take(ROUNDS))
    west_in = take(ROUNDS)
    east_in = take(ROUNDS)
    corner_in = take(ROUNDS)
    raw, raw_in, smooth, mat, weights, load_sem, send_sem, recv_sem = take(8)
    WEST, EAST = 0, 1

    me_in = lax.axis_index("inline")
    me_x = lax.axis_index("xline")
    n_in = lax.axis_size("inline")
    n_x = lax.axis_size("xline")
    has = {
        (-1, 0): me_in > 0,
        (1, 0): me_in < n_in - 1,
        (0, -1): me_x > 0,
        (0, 1): me_x < n_x - 1,
    }
    for di, dx in WAYS[4:]:
        has[(di, dx)] = jnp.logical_and(has[(di, 0)], has[(0, dx)])

    def device(way):
        return {"inline": me_in + way[0], "xline": me_x + way[1]}

    loads = [
        pltpu.make_async_copy(diffusion, raw, load_sem.at[0]),
        pltpu.make_async_copy(probes.at[0], xs[0].at[1, H:H + I, 0:J], load_sem.at[1]),
        pltpu.make_async_copy(probes.at[1], xs[0].at[0, H:H + I, 0:J], load_sem.at[2]),
        pltpu.make_async_copy(wavelet, weights, load_sem.at[3]),
    ]
    for load in loads:
        load.start()

    barrier = pltpu.get_barrier_semaphore()
    for way in WAYS:
        @pl.when(has[way])
        def _(way=way):
            pl.semaphore_signal(
                barrier, inc=1, device_id=device(way), device_id_type=pl.DeviceIdType.MESH
            )

    for side, rows, corners, edge in (
        ((-1, 0), slice(0, H), (0, 1), 0),
        ((1, 0), slice(H + I, R), (2, 3), 1),
    ):
        @pl.when(jnp.logical_not(has[side]))
        def _(rows=rows, corners=corners, edge=edge):
            raw_in[edge] = jnp.zeros(raw_in.shape[1:], bf16)
            for r in range(ROUNDS):
                xs[r][0:VECTORS, rows, 0:J] = jnp.zeros((VECTORS, H, J, S), f32)
                for corner in corners:
                    corner_in[r][corner] = jnp.zeros(corner_in[r].shape[1:], bf16)
    for side, buffers, corners in (((0, 1), east_in, (1, 3)), ((0, -1), west_in, (0, 2))):
        @pl.when(jnp.logical_not(has[side]))
        def _(buffers=buffers, corners=corners):
            for r in range(ROUNDS):
                buffers[r][...] = jnp.zeros(buffers[r].shape, bf16)
                for corner in corners:
                    corner_in[r][corner] = jnp.zeros(corner_in[r].shape[1:], bf16)

    neighbours = (
        (1 + has[(-1, 0)].astype(jnp.int32) + has[(1, 0)].astype(jnp.int32))
        * (1 + has[(0, -1)].astype(jnp.int32) + has[(0, 1)].astype(jnp.int32))
        - 1
    )

    def planes_of(r, group):
        if group == 1:
            return (0, 1)
        return (1, PLANES) if r == 0 else (1, 2)

    def copies(r, group):
        x = xs[r]
        p = slice(*planes_of(r, group))
        vector = 1 - group
        west, east = sent_side[WEST][r], sent_side[EAST][r]
        count = I * H
        first, final = slice(0, TILE), slice(count - TILE, count)
        ends = [
            ((-1, 0), x.at[vector, H:2 * H, 0:J], x.at[vector, H + I:R, 0:J]),
            ((1, 0), x.at[vector, I:I + H, 0:J], x.at[vector, 0:H, 0:J]),
            ((0, -1), west.at[p], east_in[r].at[p]),
            ((0, 1), east.at[p], west_in[r].at[p]),
            ((-1, -1), west.at[p, first], corner_in[r].at[3, p]),
            ((-1, 1), east.at[p, first], corner_in[r].at[2, p]),
            ((1, -1), west.at[p, final], corner_in[r].at[1, p]),
            ((1, 1), east.at[p, final], corner_in[r].at[0, p]),
        ]
        if r == 0 and group == 0:
            ends += [
                ((-1, 0), raw.at[:, 0:H], raw_in.at[1]),
                ((1, 0), raw.at[:, I - H:I], raw_in.at[0]),
            ]
        return [
            (
                way,
                pltpu.make_async_remote_copy(
                    src_ref=source,
                    dst_ref=target,
                    send_sem=send_sem.at[r, group, k],
                    recv_sem=recv_sem.at[r, group, k],
                    device_id=device(way),
                    device_id_type=pl.DeviceIdType.MESH,
                ),
            )
            for k, (way, source, target) in enumerate(ends)
        ]

    def send(r, group):
        for p in range(*planes_of(r, group)):
            for side in (WEST, EAST):
                sent_side[side][r][p] = made_side[side][p].astype(bf16)
        for way, copy in copies(r, group):
            @pl.when(has[way])
            def _(copy=copy):
                copy.start()

    def pack(planes):
        for p in range(*planes):
            for i in range(I):
                made_side[WEST][p, i * H:(i + 1) * H] = xs[0][p, H + i, 0:H]
                made_side[EAST][p, i * H:(i + 1) * H] = xs[0][p, H + i, J - H:J]

    def receive(r, group):
        for way, copy in copies(r, group):
            @pl.when(has[(-way[0], -way[1])])
            def _(copy=copy):
                copy.wait_recv()
        x = xs[r]
        if r == 0 and group == 0:
            for edge, row in ((0, 0), (1, H + I)):
                x[VECTORS:PLANES, row:row + H, 0:J] = raw_in[edge].astype(f32) * DAMPING
        for p in range(*planes_of(r, group)):
            for column, middle, north, south in (
                (J, east_in[r], 1, 3),
                (C - H, west_in[r], 0, 2),
            ):
                main = middle[p].astype(f32)
                upper = corner_in[r][north, p].astype(f32)
                lower = corner_in[r][south, p].astype(f32)
                for i in range(I):
                    x[p, H + i, column:column + H] = main[i * H:(i + 1) * H]
                for i in range(H):
                    start = TILE - H * H + i * H
                    x[p, i, column:column + H] = upper[start:start + H]
                    x[p, H + I + i, column:column + H] = lower[i * H:(i + 1) * H]

    def product(block):
        top = block.astype(bf16)
        rest = (block - top.astype(f32)).astype(bf16)
        both = jnp.dot(
            jnp.concatenate([top, rest], axis=1), mat[...], preferred_element_type=f32
        )
        return both[:, :S] + both[:, S:]

    def smooth_own(src, plane):
        block = src[plane, H:H + I, 0:J].reshape(I * J, S)
        smooth[plane, H:H + I, 0:J] = product(block).reshape(I, J, S)

    def smooth_rest(src, plane, low, high):
        before, after = H - low, high - H - I
        pieces = [
            src[plane, low:H, 0:J].reshape(before * J, S),
            src[plane, H + I:high, 0:J].reshape(after * J, S),
            src[plane, low:high, J:C].reshape((high - low) * SUB, S),
        ]
        result = product(jnp.concatenate(pieces, axis=0))
        a, b = before * J, (before + after) * J
        smooth[plane, low:H, 0:J] = result[:a].reshape(before, J, S)
        smooth[plane, H + I:high, 0:J] = result[a:b].reshape(after, J, S)
        smooth[plane, low:high, J:C] = result[b:].reshape(high - low, SUB, S)

    def stencil(src, plane, low, high, store):
        tensor = xs[0]

        def flux(i, here):
            below = src[plane, i + 1]
            a, b, c = tensor[VECTORS, i], tensor[VECTORS + 1, i], tensor[VECTORS + 2, i]
            step_in = below - here
            step_x = pltpu.roll(here, C - 1, axis=0) - here
            return below, a * step_in + b * step_x, b * step_in + c * step_x

        here, above, _ = flux(low - 1, src[plane, low - 1])
        for i in range(low, high):
            below, flux_in, flux_x = flux(i, here)
            regular = (above - flux_in) + (pltpu.roll(flux_x, 1, axis=0) - flux_x)
            store(i, regular)
            here, above = below, flux_in

    loads[0].wait()
    for q in range(3):
        xs[0][VECTORS + q, H:H + I, 0:J] = raw[q].astype(f32) * DAMPING
    loads[1].wait()
    pack(planes_of(0, 0))
    pl.semaphore_wait(barrier, neighbours)
    send(0, 0)
    loads[2].wait()
    pack(planes_of(0, 1))
    send(0, 1)
    row = lax.broadcasted_iota(jnp.int32, (S, S), 0)
    col = lax.broadcasted_iota(jnp.int32, (S, S), 1)
    taps = wavelet.shape[0]
    offset = col - row + taps // 2
    loads[3].wait()
    band = jnp.zeros((S, S), f32)
    for k in range(taps):
        band = jnp.where(offset == k, weights[k], band)
    gram = lax.dot_general(
        band, band, (((1,), (1,)), ((), ())),
        precision=lax.Precision.HIGHEST, preferred_element_type=f32,
    )
    whole = jnp.where(row == col, f32(1.0), f32(0.0)) - DAMPING * gram
    top = whole.astype(bf16)
    rest = (whole - top.astype(f32)).astype(bf16)
    for k in range(2):
        mat[k * S:(k + 1) * S, 0:S] = top
        mat[k * S:(k + 1) * S, S:2 * S] = rest

    for group in range(2):
        smooth_own(xs[0], 1 - group)
    for r in range(ROUNDS):
        for group in range(2):
            plane = 1 - group
            receive(r, group)
            src = xs[r]
            for k in range(1, H + 1):
                extra = H - k
                low, high = H - extra, H + I + extra
                last = k == H
                if k > 1:
                    smooth_own(src, plane)
                if not last:
                    smooth_rest(src, plane, low, high)
                    dst = ys[r * (H - 1) + k - 1]

                    def store(i, regular):
                        dst[plane, i] = smooth[plane, i] - regular
                else:
                    def store(i, regular):
                        value = smooth[plane, i, 0:J] - regular[0:J]
                        if r == ROUNDS - 1:
                            out[group, i - H] = value
                            return
                        xs[r + 1][plane, i, 0:J] = value
                        place = slice((i - H) * H, (i - H + 1) * H)
                        made_side[WEST][plane, place] = value[0:H]
                        made_side[EAST][plane, place] = value[J - H:J]
                stencil(src, plane, low, high, store)
                if not last:
                    @pl.when(jnp.logical_not(has[(1, 0)]))
                    def _():
                        dst[plane, H + I:high] = jnp.zeros((extra, C, S), f32)

                    @pl.when(jnp.logical_not(has[(0, 1)]))
                    def _():
                        dst[plane, low:high, J:J + extra] = jnp.zeros((high - low, extra, S), f32)
                    src = dst
            if r < ROUNDS - 1:
                send(r + 1, group)
                smooth_own(xs[r + 1], plane)

    for r in range(ROUNDS):
        for group in range(2):
            for way, copy in copies(r, group):
                @pl.when(has[way])
                def _(copy=copy):
                    copy.wait_send()


def per_device(probes, diffusion, wavelet):
    nv, I, J, S = probes.shape
    H = WIDTH
    C = J + SUB
    R = I + 2 * H
    f32 = jnp.float32
    planes = [PLANES] + [VECTORS] * (ROUNDS - 1)
    bf16 = jnp.bfloat16
    scratch = (
        [pltpu.VMEM((p, R, C, S), f32) for p in planes]
        + [pltpu.VMEM((VECTORS, R, C, S), f32) for _ in range(ROUNDS * (H - 1))]
        + [pltpu.VMEM((PLANES, I * H, S), f32)] * 2
        + [pltpu.VMEM((p, I * H, S), bf16) for p in planes] * 4
        + [pltpu.VMEM((4, p, TILE, S), bf16) for p in planes]
        + [
            pltpu.VMEM(diffusion.shape, diffusion.dtype),
            pltpu.VMEM((2, 3, H, J, S), bf16),
            pltpu.VMEM((VECTORS, R, C, S), f32),
            pltpu.VMEM((2 * S, 2 * S), bf16),
            pltpu.SMEM(wavelet.shape, f32),
            pltpu.SemaphoreType.DMA((4,)),
            pltpu.SemaphoreType.DMA((ROUNDS, 2, len(WAYS) + 2)),
            pltpu.SemaphoreType.DMA((ROUNDS, 2, len(WAYS) + 2)),
        ]
    )
    return pl.pallas_call(
        kernel,
        out_shape=jax.ShapeDtypeStruct(probes.shape, f32),
        in_specs=[
            pl.BlockSpec(memory_space=pltpu.HBM),
            pl.BlockSpec(memory_space=pltpu.HBM),
            pl.BlockSpec(memory_space=pltpu.HBM),
        ],
        out_specs=pl.BlockSpec(memory_space=pltpu.VMEM),
        scratch_shapes=scratch,
        compiler_params=pltpu.CompilerParams(
            collective_id=0, has_side_effects=True, vmem_limit_bytes=32 * 1024 * 1024
        ),
        cost_estimate=pl.CostEstimate(flops=STEPS * 2 * 1024 * 256 * 256, bytes_accessed=1500000, transcendentals=0),
    )(probes, diffusion, wavelet)


def solution(mesh):
    return jax.shard_map(
        per_device,
        mesh=mesh,
        in_specs=(P(None, "inline", "xline", None), P(None, "inline", "xline", None), P()),
        out_specs=P(None, "inline", "xline", None),
        check_vma=False,
    )
```

time: 27.7 us -> 23.9 us (0.86)
  Pallas kernels: 24 us -> 20.2 us
    pallas_call x1, Pallas kernels: 24 us -> 20.2 us  [per_device(): pl.pallas_call(kernel, out_shape=jax.ShapeDtypeStruct(probes.shape, f32),...]
where the time goes in v2:
time: 23.9 us; the launch traced here: 23.7 us
  Pallas kernels  20.2 us (85%)
  local copies, waits for them, and re-layouts  3.49 us (15%)
    pallas_call x1, Pallas kernels, per_device(): pl.pallas_call(kernel, out_shape=jax.ShapeDtypeStruct(probes.shape, f32),...  20.2 us
    unnamed x7, local copies, waits for them, and re-layouts  3.49 us

profile of v2, /device:TPU:1, one launch (start us, length us, event | category | flops | bytes accessed | tf_op | source)
XLA Modules:
  0.0 23.7 jit_solution(13472998657741643878)
XLA Ops:
  0.0 0.0 copy-start
  0.0 1.0 %copy-done = f32[2,16,32,128]{3,2,1,0:T(8,128)S(1)} copy-done((f32[2,16,32,128]{3,2,1,0:T(8,128)S(1)}, f32[2,16,32,128]{3,2,1,0:T(8,128)}, u32[]{:S(2)}) %copy-start) | copy-done | bytes 524312
  1.0 0.0 copy-start.1
  1.0 1.0 %copy-done.1 = bf16[3,16,32,128]{3,2,1,0:T(8,128)(2,1)S(1)} copy-done((bf16[3,16,32,128]{3,2,1,0:T(8,128)(2,1)S(1)}, bf16[3,16,32,128]{3,2,1,0:T(8,128)(2,1)}, u32[]{:S(2)}) %copy-start.1) | copy-done | bytes 393240
  2.0 0.0 copy-start.2
  2.0 0.7 %copy-done.2 = f32[41]{0:T(128)S(1)} copy-done((f32[41]{0:T(128)S(1)}, f32[41]{0:T(128)}, u32[]{:S(2)}) %copy-start.2) | copy-done | bytes 188
  2.7 20.2 %shard_map.37 = f32[2,16,32,128]{3,2,1,0:T(8,128)S(1)} custom-call(f32[2,16,32,128]{3,2,1,0:T(8,128)S(1)} %copy-done, bf16[3,16,32,128]{3,2,1,0:T(8,128)(2,1)S(1)} %copy-done.1, f32[41]{0:T(128)S(1)} %copy-done.2), custom_call_target="tpu_custom_call" | custom-call | flops 805306368 | bytes 1500000 | tf_op jit(solution)/shard_map/pallas_call | solution.py:330
  22.9 0.8 %copy.5 = f32[2,16,32,128]{3,2,1,0:T(8,128)} copy(f32[2,16,32,128]{3,2,1,0:T(8,128)S(1)} %shard_map.37) | data formatting | bytes 1048576
Async XLA Ops:
  0.0 1.0 %copy-start = (f32[2,16,32,128]{3,2,1,0:T(8,128)S(1)}, f32[2,16,32,128]{3,2,1,0:T(8,128)}, u32[]{:S(2)}) copy-start(f32[2,16,32,128]{3,2,1,0:T(8,128)} %probes.1) | copy-start | bytes 1572868
  1.0 1.0 %copy-start.1 = (bf16[3,16,32,128]{3,2,1,0:T(8,128)(2,1)S(1)}, bf16[3,16,32,128]{3,2,1,0:T(8,128)(2,1)}, u32[]{:S(2)}) copy-start(bf16[3,16,32,128]{3,2,1,0:T(8,128)(2,1)} %diffusion.1) | copy-start | bytes 1179652
  2.0 0.7 %copy-start.2 = (f32[41]{0:T(128)S(1)}, f32[41]{0:T(128)}, u32[]{:S(2)}) copy-start(f32[41]{0:T(128)} %wavelet.1) | copy-start | bytes 496

commit v3 on v2

--- a/solution.py
+++ b/solution.py
@@ -8,7 +8,7 @@
 from jax.sharding import PartitionSpec as P
 
 STEPS = 6
-WIDTH = 2
+WIDTH = 3
 ROUNDS = STEPS // WIDTH
 DAMPING = 0.25
 VECTORS = 2
@@ -74,25 +74,6 @@
                 barrier, inc=1, device_id=device(way), device_id_type=pl.DeviceIdType.MESH
             )
 
-    for side, rows, corners, edge in (
-        ((-1, 0), slice(0, H), (0, 1), 0),
-        ((1, 0), slice(H + I, R), (2, 3), 1),
-    ):
-        @pl.when(jnp.logical_not(has[side]))
-        def _(rows=rows, corners=corners, edge=edge):
-            raw_in[edge] = jnp.zeros(raw_in.shape[1:], bf16)
-            for r in range(ROUNDS):
-                xs[r][0:VECTORS, rows, 0:J] = jnp.zeros((VECTORS, H, J, S), f32)
-                for corner in corners:
-                    corner_in[r][corner] = jnp.zeros(corner_in[r].shape[1:], bf16)
-    for side, buffers, corners in (((0, 1), east_in, (1, 3)), ((0, -1), west_in, (0, 2))):
-        @pl.when(jnp.logical_not(has[side]))
-        def _(buffers=buffers, corners=corners):
-            for r in range(ROUNDS):
-                buffers[r][...] = jnp.zeros(buffers[r].shape, bf16)
-                for corner in corners:
-                    corner_in[r][corner] = jnp.zeros(corner_in[r].shape[1:], bf16)
-
     neighbours = (
         (1 + has[(-1, 0)].astype(jnp.int32) + has[(1, 0)].astype(jnp.int32))
         * (1 + has[(0, -1)].astype(jnp.int32) + has[(0, 1)].astype(jnp.int32))
@@ -112,14 +93,14 @@
         count = I * H
         first, final = slice(0, TILE), slice(count - TILE, count)
         ends = [
-            ((-1, 0), x.at[vector, H:2 * H, 0:J], x.at[vector, H + I:R, 0:J]),
-            ((1, 0), x.at[vector, I:I + H, 0:J], x.at[vector, 0:H, 0:J]),
-            ((0, -1), west.at[p], east_in[r].at[p]),
-            ((0, 1), east.at[p], west_in[r].at[p]),
             ((-1, -1), west.at[p, first], corner_in[r].at[3, p]),
             ((-1, 1), east.at[p, first], corner_in[r].at[2, p]),
             ((1, -1), west.at[p, final], corner_in[r].at[1, p]),
             ((1, 1), east.at[p, final], corner_in[r].at[0, p]),
+            ((0, -1), west.at[p], east_in[r].at[p]),
+            ((0, 1), east.at[p], west_in[r].at[p]),
+            ((-1, 0), x.at[vector, H:2 * H, 0:J], x.at[vector, H + I:R, 0:J]),
+            ((1, 0), x.at[vector, I:I + H, 0:J], x.at[vector, 0:H, 0:J]),
         ]
         if r == 0 and group == 0:
             ends += [
@@ -232,6 +213,25 @@
     loads[2].wait()
     pack(planes_of(0, 1))
     send(0, 1)
+    for side, rows, corners, edge in (
+        ((-1, 0), slice(0, H), (0, 1), 0),
+        ((1, 0), slice(H + I, R), (2, 3), 1),
+    ):
+        @pl.when(jnp.logical_not(has[side]))
+        def _(rows=rows, corners=corners, edge=edge):
+            raw_in[edge] = jnp.zeros(raw_in.shape[1:], bf16)
+            for r in range(ROUNDS):
+                xs[r][0:VECTORS, rows, 0:J] = jnp.zeros((VECTORS, H, J, S), f32)
+                for corner in corners:
+                    corner_in[r][corner] = jnp.zeros(corner_in[r].shape[1:], bf16)
+    for side, buffers, corners in (((0, 1), east_in, (1, 3)), ((0, -1), west_in, (0, 2))):
+        @pl.when(jnp.logical_not(has[side]))
+        def _(buffers=buffers, corners=corners):
+            for r in range(ROUNDS):
+                buffers[r][...] = jnp.zeros(buffers[r].shape, bf16)
+                for corner in corners:
+                    corner_in[r][corner] = jnp.zeros(corner_in[r].shape[1:], bf16)
+
     row = lax.broadcasted_iota(jnp.int32, (S, S), 0)
     col = lax.broadcasted_iota(jnp.int32, (S, S), 1)
     taps = wavelet.shape[0]

time: 23.9 us -> 20.1 us (0.84)
  Pallas kernels: 20.2 us -> 16.4 us
    pallas_call x1, Pallas kernels: 20.2 us -> 16.4 us  [per_device(): pl.pallas_call(kernel, out_shape=jax.ShapeDtypeStruct(probes.shape, f32),...]
where the time goes in v3:
time: 20.1 us; the launch traced here: 19.9 us
  Pallas kernels  16.4 us (82%)
  local copies, waits for them, and re-layouts  3.49 us (17%)
    pallas_call x1, Pallas kernels, per_device(): pl.pallas_call(kernel, out_shape=jax.ShapeDtypeStruct(probes.shape, f32),...  16.4 us
    unnamed x7, local copies, waits for them, and re-layouts  3.49 us

profile of v3, /device:TPU:1, one launch (start us, length us, event | category | flops | bytes accessed | tf_op | source)
XLA Modules:
  0.0 19.9 jit_solution(2257146796533671067)
XLA Ops:
  0.0 0.0 copy-start
  0.0 1.0 %copy-done = f32[2,16,32,128]{3,2,1,0:T(8,128)S(1)} copy-done((f32[2,16,32,128]{3,2,1,0:T(8,128)S(1)}, f32[2,16,32,128]{3,2,1,0:T(8,128)}, u32[]{:S(2)}) %copy-start) | copy-done | bytes 524312
  1.0 0.0 copy-start.1
  1.0 1.0 %copy-done.1 = bf16[3,16,32,128]{3,2,1,0:T(8,128)(2,1)S(1)} copy-done((bf16[3,16,32,128]{3,2,1,0:T(8,128)(2,1)S(1)}, bf16[3,16,32,128]{3,2,1,0:T(8,128)(2,1)}, u32[]{:S(2)}) %copy-start.1) | copy-done | bytes 393240
  2.0 0.0 copy-start.2
  2.0 0.7 %copy-done.2 = f32[41]{0:T(128)S(1)} copy-done((f32[41]{0:T(128)S(1)}, f32[41]{0:T(128)}, u32[]{:S(2)}) %copy-start.2) | copy-done | bytes 188
  2.7 16.4 %shard_map.37 = f32[2,16,32,128]{3,2,1,0:T(8,128)S(1)} custom-call(f32[2,16,32,128]{3,2,1,0:T(8,128)S(1)} %copy-done, bf16[3,16,32,128]{3,2,1,0:T(8,128)(2,1)S(1)} %copy-done.1, f32[41]{0:T(128)S(1)} %copy-done.2), custom_call_target="tpu_custom_call" | custom-call | flops 805306368 | bytes 1500000 | tf_op jit(solution)/shard_map/pallas_call | solution.py:330
  19.1 0.8 %copy.5 = f32[2,16,32,128]{3,2,1,0:T(8,128)} copy(f32[2,16,32,128]{3,2,1,0:T(8,128)S(1)} %shard_map.37) | data formatting | bytes 1048576
Async XLA Ops:
  0.0 1.0 %copy-start = (f32[2,16,32,128]{3,2,1,0:T(8,128)S(1)}, f32[2,16,32,128]{3,2,1,0:T(8,128)}, u32[]{:S(2)}) copy-start(f32[2,16,32,128]{3,2,1,0:T(8,128)} %probes.1) | copy-start | bytes 1572868
  1.0 1.0 %copy-start.1 = (bf16[3,16,32,128]{3,2,1,0:T(8,128)(2,1)S(1)}, bf16[3,16,32,128]{3,2,1,0:T(8,128)(2,1)}, u32[]{:S(2)}) copy-start(bf16[3,16,32,128]{3,2,1,0:T(8,128)(2,1)} %diffusion.1) | copy-start | bytes 1179652
  2.0 0.7 %copy-start.2 = (f32[41]{0:T(128)S(1)}, f32[41]{0:T(128)}, u32[]{:S(2)}) copy-start(f32[41]{0:T(128)} %wavelet.1) | copy-start | bytes 496

commit v4 on v3

--- a/solution.py
+++ b/solution.py
@@ -57,6 +57,14 @@
     def device(way):
         return {"inline": me_in + way[0], "xline": me_x + way[1]}
 
+    barrier = pltpu.get_barrier_semaphore()
+    for way in WAYS[4:] + WAYS[:4]:
+        @pl.when(has[way])
+        def _(way=way):
+            pl.semaphore_signal(
+                barrier, inc=1, device_id=device(way), device_id_type=pl.DeviceIdType.MESH
+            )
+
     loads = [
         pltpu.make_async_copy(diffusion, raw, load_sem.at[0]),
         pltpu.make_async_copy(probes.at[0], xs[0].at[1, H:H + I, 0:J], load_sem.at[1]),
@@ -65,14 +73,6 @@
     ]
     for load in loads:
         load.start()
-
-    barrier = pltpu.get_barrier_semaphore()
-    for way in WAYS:
-        @pl.when(has[way])
-        def _(way=way):
-            pl.semaphore_signal(
-                barrier, inc=1, device_id=device(way), device_id_type=pl.DeviceIdType.MESH
-            )
 
     neighbours = (
         (1 + has[(-1, 0)].astype(jnp.int32) + has[(1, 0)].astype(jnp.int32))
@@ -138,24 +138,31 @@
                 made_side[EAST][p, i * H:(i + 1) * H] = xs[0][p, H + i, J - H:J]
 
     def receive(r, group):
-        for way, copy in copies(r, group):
-            @pl.when(has[(-way[0], -way[1])])
-            def _(copy=copy):
-                copy.wait_recv()
+        arriving = copies(r, group)
+
+        def wait(part):
+            for way, copy in part:
+                @pl.when(has[(-way[0], -way[1])])
+                def _(copy=copy):
+                    copy.wait_recv()
+
         x = xs[r]
+        sides = ((J, east_in[r], 1, 3), (C - H, west_in[r], 0, 2))
+        wait(arriving[6:])
         if r == 0 and group == 0:
             for edge, row in ((0, 0), (1, H + I)):
                 x[VECTORS:PLANES, row:row + H, 0:J] = raw_in[edge].astype(f32) * DAMPING
+        wait(arriving[4:6])
         for p in range(*planes_of(r, group)):
-            for column, middle, north, south in (
-                (J, east_in[r], 1, 3),
-                (C - H, west_in[r], 0, 2),
-            ):
+            for column, middle, north, south in sides:
                 main = middle[p].astype(f32)
+                for i in range(I):
+                    x[p, H + i, column:column + H] = main[i * H:(i + 1) * H]
+        wait(arriving[:4])
+        for p in range(*planes_of(r, group)):
+            for column, middle, north, south in sides:
                 upper = corner_in[r][north, p].astype(f32)
                 lower = corner_in[r][south, p].astype(f32)
-                for i in range(I):
-                    x[p, H + i, column:column + H] = main[i * H:(i + 1) * H]
                 for i in range(H):
                     start = TILE - H * H + i * H
                     x[p, i, column:column + H] = upper[start:start + H]

time: 20.1 us -> 19.9 us (0.990)
    pallas_call x1, Pallas kernels: 16.4 us -> 16.2 us  [per_device(): pl.pallas_call(kernel, out_shape=jax.ShapeDtypeStruct(probes.shape, f32),...]
where the time goes in v4:
time: 19.9 us; the launch traced here: 19.7 us
  Pallas kernels  16.2 us (81%)
  local copies, waits for them, and re-layouts  3.49 us (18%)
    pallas_call x1, Pallas kernels, per_device(): pl.pallas_call(kernel, out_shape=jax.ShapeDtypeStruct(probes.shape, f32),...  16.2 us
    unnamed x7, local copies, waits for them, and re-layouts  3.49 us

profile of v4, /device:TPU:1, one launch (start us, length us, event | category | flops | bytes accessed | tf_op | source)
XLA Modules:
  0.0 19.7 jit_solution(1542763552194277172)
XLA Ops:
  0.0 0.0 copy-start
  0.0 1.0 %copy-done = f32[2,16,32,128]{3,2,1,0:T(8,128)S(1)} copy-done((f32[2,16,32,128]{3,2,1,0:T(8,128)S(1)}, f32[2,16,32,128]{3,2,1,0:T(8,128)}, u32[]{:S(2)}) %copy-start) | copy-done | bytes 524312
  1.0 0.0 copy-start.1
  1.0 1.0 %copy-done.1 = bf16[3,16,32,128]{3,2,1,0:T(8,128)(2,1)S(1)} copy-done((bf16[3,16,32,128]{3,2,1,0:T(8,128)(2,1)S(1)}, bf16[3,16,32,128]{3,2,1,0:T(8,128)(2,1)}, u32[]{:S(2)}) %copy-start.1) | copy-done | bytes 393240
  2.0 0.0 copy-start.2
  2.0 0.7 %copy-done.2 = f32[41]{0:T(128)S(1)} copy-done((f32[41]{0:T(128)S(1)}, f32[41]{0:T(128)}, u32[]{:S(2)}) %copy-start.2) | copy-done | bytes 188
  2.7 16.2 %shard_map.37 = f32[2,16,32,128]{3,2,1,0:T(8,128)S(1)} custom-call(f32[2,16,32,128]{3,2,1,0:T(8,128)S(1)} %copy-done, bf16[3,16,32,128]{3,2,1,0:T(8,128)(2,1)S(1)} %copy-done.1, f32[41]{0:T(128)S(1)} %copy-done.2), custom_call_target="tpu_custom_call" | custom-call | flops 805306368 | bytes 1500000 | tf_op jit(solution)/shard_map/pallas_call | solution.py:337
  18.9 0.8 %copy.5 = f32[2,16,32,128]{3,2,1,0:T(8,128)} copy(f32[2,16,32,128]{3,2,1,0:T(8,128)S(1)} %shard_map.37) | data formatting | bytes 1048576
Async XLA Ops:
  0.0 1.0 %copy-start = (f32[2,16,32,128]{3,2,1,0:T(8,128)S(1)}, f32[2,16,32,128]{3,2,1,0:T(8,128)}, u32[]{:S(2)}) copy-start(f32[2,16,32,128]{3,2,1,0:T(8,128)} %probes.1) | copy-start | bytes 1572868
  1.0 1.0 %copy-start.1 = (bf16[3,16,32,128]{3,2,1,0:T(8,128)(2,1)S(1)}, bf16[3,16,32,128]{3,2,1,0:T(8,128)(2,1)}, u32[]{:S(2)}) copy-start(bf16[3,16,32,128]{3,2,1,0:T(8,128)(2,1)} %diffusion.1) | copy-start | bytes 1179652
  2.0 0.7 %copy-start.2 = (f32[41]{0:T(128)S(1)}, f32[41]{0:T(128)}, u32[]{:S(2)}) copy-start(f32[41]{0:T(128)} %wavelet.1) | copy-start | bytes 496
